TPU v7x, 32 devices: a whole 2x2x4 slice. The times are simulated.
32 devices in a mesh: dp: 2 (over core), wide: 8 (over z, y), narrow: 2 (over x).
Axes of the slice: x: 2, y: 2, z: 4, core: 2. Of those that a mesh axis runs over, the one named last changes fastest.
Arguments:
- layer_input: bfloat16 [8192, 1088], P(('dp', 'wide'), 'narrow'), may hold values from -6 to 6
- doc_segments: int32 [2, 4096], replicated, may hold values from 0 to 7, as said below
- first_gain: bfloat16 [1088], P('narrow'), may hold values from 0.25 to 1.75
- first_shift: bfloat16 [1088], P('narrow'), may hold values from -2 to 2
- heads_weight: bfloat16 [1088, 3, 1088], P('narrow', None, 'wide'), may hold values from -1 to 1
- query_bias: bfloat16 [1088], P('wide'), may hold values from -2 to 2
- value_bias: bfloat16 [1088], P('wide'), may hold values from -2 to 2
- merge_weight: bfloat16 [1088, 1088], P('wide', 'narrow'), may hold values from -0.1875 to 0.1875
- merge_bias: bfloat16 [1088], P('narrow'), may hold values from -2 to 2
- second_gain: bfloat16 [1088], P('narrow'), may hold values from 0.25 to 1.75
- second_shift: bfloat16 [1088], P('narrow'), may hold values from -2 to 2
- up_weight: bfloat16 [1088, 4352], P('narrow', 'wide'), may hold values from -1 to 1
- up_bias: bfloat16 [4352], P('wide'), may hold values from -2 to 2
- down_weight: bfloat16 [4352, 1088], P('wide', 'narrow'), may hold values from -0.09375 to 0.09375
- down_bias: bfloat16 [1088], P('narrow'), may hold values from -2 to 2
- out_cotangent: bfloat16 [8192, 1088], P(('dp', 'wide'), 'narrow'), may hold values from -6 to 6
Outputs:
- layer_output: bfloat16 [8192, 1088], P(('dp', 'wide'), 'narrow')
- input_grad: bfloat16 [8192, 1088], P(('dp', 'wide'), 'narrow')
- first_gain_grad: float32 [1088], P('narrow')
- first_shift_grad: float32 [1088], P('narrow')
- heads_weight_grad: float32 [1088, 3, 1088], P('narrow', None, 'wide')
- query_bias_grad: float32 [1088], P('wide')
- value_bias_grad: float32 [1088], P('wide')
- merge_weight_grad: float32 [1088, 1088], P('wide', 'narrow')
- merge_bias_grad: float32 [1088], P('narrow')
- second_gain_grad: float32 [1088], P('narrow')
- second_shift_grad: float32 [1088], P('narrow')
- up_weight_grad: float32 [1088, 4352], P('narrow', 'wide')
- up_bias_grad: float32 [4352], P('wide')
- down_weight_grad: float32 [4352, 1088], P('wide', 'narrow')
- down_bias_grad: float32 [1088], P('narrow')
Inputs may be any that keep to these rules, and one draw needn't show every extreme that they name: `doc_segments`: in each sequence's row, numbers rise by one at each document's start and every number is used; each run of 4096 positions from the row's start holds 8 whole documents, three of them of exactly 1024 tokens, and no document is longer.
All inputs are finite; a program needn't handle non-finite values.
Results may differ from a plain program's by a relative error of at most 0.0228.
The roundings to bfloat16 on the way count: a program that leaves them out, or rounds other values in their place, can miss the bound.
Values may be sent and summed in bfloat16 or wider, within the bound.
A program may use at most 320 MiB of HBM per device.

v0:
```python
import functools

import jax
import jax.numpy as jnp
from jax import lax
from jax.experimental import pallas as pl
from jax.experimental.pallas import tpu as pltpu
from jax.sharding import PartitionSpec as P

HEAD = 64
REACH = 4
EPS = 1e-05
NEGATIVE = -1e30
LANES = 128
BF = jnp.bfloat16
F32 = jnp.float32
MESH = pl.DeviceIdType.MESH
ANY = pl.BlockSpec(memory_space=pl.ANY)
DMA = pltpu.SemaphoreType.DMA
SCALE = HEAD ** (-0.5)
LIMIT = 62 * 1024 * 1024


def widths(half):
    main = half // LANES * LANES
    return main, half - main


def rem_rows(rows, half):
    main, rem = widths(half)
    return up16(-(-rows // (main // rem)))


def up16(rows):
    return -(-rows // 16) * 16


def pack(block, column=None):
    rows, half = block.shape[-2:]
    main, rem = widths(half)
    count = main // rem
    extra = rem_rows(rows, half)
    lead = block.shape[:-2]
    none = [(0, 0)] * len(lead)
    tail = jnp.pad(block[..., main:], none + [(0, count * extra - rows), (0, 0)])
    tail = jnp.swapaxes(tail.reshape(lead + (count, extra, rem)), -2, -3).reshape(lead + (extra, main))
    if column is not None:
        base, groups = column_base(rows, half), -(-rows // extra)
        column = jnp.pad(column, (0, groups * extra - rows)).reshape(groups, extra).T
        tail = jnp.concatenate([tail[:, :base], column, tail[:, base + groups :]], 1)
    return jnp.concatenate([block[..., :main], tail], -2)


def column_base(rows, half):
    return -(-rows // rem_rows(rows, half)) * widths(half)[1]


def column_of(block, rows, half):
    base, extra = column_base(rows, half), rem_rows(rows, half)
    groups = -(-rows // extra)
    tail = block[..., rows : rows + extra, base : base + groups]
    return jnp.swapaxes(tail, -1, -2).reshape(block.shape[:-2] + (groups * extra,))[..., :rows]


def unpack(block, rows, half):
    main, rem = widths(half)
    count = main // rem
    extra = rem_rows(rows, half)
    lead = block.shape[:-2]
    tail = block[..., rows : rows + extra, :].reshape(lead + (extra, count, rem))
    tail = jnp.swapaxes(tail, -2, -3).reshape(lead + (count * extra, rem))[..., :rows, :]
    return block[..., :rows, :], tail


def unpack_half(block, rows, half):
    return jnp.concatenate(unpack(block, rows, half), -1)


def join(blocks, rows, half):
    body, tail = unpack(blocks, rows, half)
    return jnp.concatenate([body[0], body[1], tail[0], tail[1]], -1)


def halves(full):
    half = full.shape[-1] // 2
    main, rem = widths(half)
    edge = 2 * main
    return jnp.stack(
        [
            jnp.concatenate([full[..., :main], full[..., edge : edge + rem]], -1),
            jnp.concatenate([full[..., main:edge], full[..., edge + rem :]], -1),
        ]
    )


def place():
    c, w, n = lax.axis_index("dp"), lax.axis_index("wide"), lax.axis_index("narrow")
    z, y = lax.div(w, 2), lax.rem(w, 2)
    first = (y + c * (1 - 2 * y), n + (1 - c) * (1 - 2 * n))
    second = (y + (1 - c) * (1 - 2 * y), n + c * (1 - 2 * n))
    return c, z, y, n, first, second


def wide_of(z, y):
    return z * 2 + y


def remote(src, dst, send, recv, device):
    return pltpu.make_async_remote_copy(
        src_ref=src, dst_ref=dst, send_sem=send, recv_sem=recv, device_id=device, device_id_type=MESH
    )


def greet(devices):
    barrier = pltpu.get_barrier_semaphore()
    for device in devices:
        pl.semaphore_signal(barrier, inc=1, device_id=device, device_id_type=MESH)
    pl.semaphore_wait(barrier, len(devices))


def partners(outer):
    c, z, y, n, _, _ = place()
    out = [(c, wide_of(lax.rem(z + d, outer), y), n) for d in range(1, outer)]
    out.append((c, wide_of(z, 1 - y), n))
    out.append((c, wide_of(z, y), 1 - n))
    out.append((1 - c, wide_of(z, y), n))
    return out


class Gather:
    def __init__(self, outer, src, out, both, first, second, sems, part=None):
        self.outer, self.src, self.out, self.both = outer, src, out, both
        self.part = outer if part is None else part
        self.first, self.second = first, second
        self.zs, self.zr, self.fs, self.fr, self.ss, self.sr, self.cs, self.cr, self.local = sems
        self.sent = []

    def block(self, z, y, n):
        c = lax.axis_index("dp")
        return self.out.at[c, wide_of(z, y), n] if self.both else self.out.at[wide_of(z, y), n]

    def go(self, copy):
        copy.start()
        self.sent.append(copy)

    def z_at(self, d):
        return lax.rem(place()[1] + self.outer - d, self.outer)

    def to_first(self, d, src):
        c, z, y, n, _, _ = place()
        first, second = self.first, self.second
        device = (c, wide_of(z, first[0]), first[1])
        self.go(remote(src, self.block(self.z_at(d), y, n), self.fs.at[d], self.fr.at[d], device))

    def to_second(self, d, src, k):
        if d >= self.part:
            return
        c, z, y, n, _, _ = place()
        first, second = self.first, self.second
        device = (c, wide_of(z, second[0]), second[1])
        dst = self.block(self.z_at(d), y, n) if k == 0 else self.block(self.z_at(d), *first)
        i = k * self.outer + d
        self.go(remote(src, dst, self.ss.at[i], self.sr.at[i], device))

    def to_core(self, i, src, dst):
        if self.both:
            c, z, y, n, _, _ = place()
            self.go(remote(src, dst, self.cs.at[i], self.cr.at[i], (1 - c, wide_of(z, y), n)))

    def start(self):
        c, z, y, n, _, _ = place()
        first, second = self.first, self.second
        own = self.block(z, y, n)
        self.keep = pltpu.make_async_copy(self.src, own, self.local)
        self.keep.start()
        for d in range(1, self.outer):
            device = (c, wide_of(lax.rem(z + d, self.outer), y), n)
            self.go(remote(self.src, own, self.zs.at[d - 1], self.zr.at[d - 1], device))

    def start_rest(self):
        c, z, y, n, _, _ = place()
        own = self.block(z, y, n)
        self.to_first(0, self.src)
        self.to_second(0, self.src, 0)
        self.to_core(0, self.src, own)

    def arrived(self, dst, recv):
        c, z, y, n, _, _ = place()
        remote(dst, dst, recv, recv, (1 - c, wide_of(z, y), n)).wait_recv()

    def along_z(self, d):
        c, z, y, n, _, _ = place()
        first, second = self.first, self.second
        got = self.block(self.z_at(d), y, n)
        self.arrived(got, self.zr.at[d - 1])
        self.to_first(d, got)
        self.to_second(d, got, 0)
        self.to_core(d, got, got)

    def along_first(self, d):
        c, z, y, n, _, _ = place()
        first, second = self.first, self.second
        got = self.block(self.z_at(d), *first)
        self.arrived(got, self.fr.at[d])
        self.to_second(d, got, 1)
        self.to_core(self.outer + d, got, got)

    def along_second(self, d, k):
        if d >= self.part:
            return
        c, z, y, n, _, _ = place()
        first, second = self.first, self.second
        got = self.block(self.z_at(d), *second) if k == 0 else self.block(self.z_at(d), 1 - y, 1 - n)
        i = k * self.outer + d
        self.arrived(got, self.sr.at[i])
        self.to_core(2 * self.outer + i, got, got)

    def finish(self):
        c, z, y, n, _, _ = place()
        first, second = self.first, self.second
        if self.both:
            spots = [(y, n), first, second, (1 - y, 1 - n)]
            for k, spot in enumerate(spots):
                for d in range(self.outer):
                    got = self.out.at[1 - c, wide_of(self.z_at(d), spot[0]), spot[1]]
                    self.arrived(got, self.cr.at[k * self.outer + d])
        self.keep.wait()
        for copy in self.sent:
            copy.wait_send()


def gather_sems(outer):
    return [
        DMA((outer,)),
        DMA((outer,)),
        DMA((outer,)),
        DMA((outer,)),
        DMA((2 * outer,)),
        DMA((2 * outer,)),
        DMA((4 * outer,)),
        DMA((4 * outer,)),
        DMA,
    ]


class Scatter:
    def __init__(self, outer, first, second, part, one, two, three, fin, sems):
        self.outer, self.part, self.first, self.second = outer, part, first, second
        self.one, self.two, self.three, self.fin = one, two, three, fin
        self.ss, self.sr, self.fs, self.fr, self.zs, self.zr, self.cs, self.cr = sems
        self.sent, self.along_first = [], {}

    def go(self, copy):
        copy.start()
        self.sent.append(copy)

    def arrived(self, dst, recv):
        c, z, y, n, _, _ = place()
        remote(dst, dst, recv, recv, (1 - c, wide_of(z, y), n)).wait_recv()

    def z_at(self, d):
        return lax.rem(place()[1] + d, self.outer)

    def order(self):
        return [d for d in range(1, self.outer)] + [0]

    def start(self, begin=0, end=None):
        c, z, y, n, _, _ = place()
        first, second = self.first, self.second
        device = (c, wide_of(z, second[0]), second[1])
        for d in self.order()[begin:end]:
            for k, spot in ((1, (1 - y, 1 - n)), (0, second)):
                i = k * self.outer + d
                self.go(
                    remote(self.part(self.z_at(d), *spot), self.one.at[i], self.ss.at[i], self.sr.at[i], device)
                )

    def steps(self):
        order = self.order()
        out = [functools.partial(self.to_first, order[0])]
        for here, there in zip(order[1:], order):
            out.append(functools.partial(self.to_first, here))
            out.append(functools.partial(self.to_z, there))
        return out + [functools.partial(self.to_z, order[-1])]

    def read(self, *refs):
        return [ref[...].astype(F32) for ref in refs]

    def to_first(self, d):
        c, z, y, n, _, _ = place()
        first, second = self.first, self.second
        device = (c, wide_of(z, first[0]), first[1])
        i = self.outer + d
        self.arrived(self.one.at[i], self.sr.at[i])
        own, got = self.read(self.part(self.z_at(d), *first), self.one.at[i])
        src = self.for_first(d)
        src[...] = (got + own).astype(BF)
        self.along_first[d] = remote(src, self.two.at[d], self.fs.at[d], self.fr.at[d], device)
        self.go(self.along_first[d])

    def for_first(self, d):
        return self.one.at[self.outer + d]

    def for_z(self, d):
        return self.one.at[d]

    def to_z(self, d):
        c, z, y, n, _, _ = place()
        self.arrived(self.one.at[d], self.sr.at[d])
        self.arrived(self.two.at[d], self.fr.at[d])
        own, one, two = self.read(self.part(self.z_at(d), y, n), self.one.at[d], self.two.at[d])
        value = (one + own).astype(BF).astype(F32) + two
        if d == 0:
            self.fin[c] = value
        else:
            src = self.for_z(d)
            src[...] = value.astype(BF)
            device = (c, wide_of(self.z_at(d), y), n)
            self.go(remote(src, self.three.at[d - 1], self.zs.at[d - 1], self.zr.at[d - 1], device))

    def close(self, edges, rem, edge_sems):
        c, z, y, n, _, _ = place()
        for d in range(1, self.outer):
            self.arrived(self.three.at[d - 1], self.zr.at[d - 1])
        value = self.fin[c]
        for d in range(1, self.outer):
            value = value + self.read(self.three.at[d - 1])[0]
        self.fin[c] = value
        other = (1 - c, wide_of(z, y), n)
        self.go(remote(self.fin.at[c], self.fin.at[c], self.cs, self.cr, other))
        rows = edges.shape[1]
        tail = value[rows:]
        base = -(-rows // tail.shape[0]) * rem
        empty = jnp.zeros((rows, LANES - rem - 1), F32)
        edges[c] = jnp.concatenate([spread(tail, rows, rem), spread(tail[:, base:], rows, 1), empty], 1)
        self.edges, self.edge_recv = edges, edge_sems.at[1]
        self.go(remote(edges.at[c], edges.at[c], edge_sems.at[0], edge_sems.at[1], other))

    def finish(self):
        c = lax.axis_index("dp")
        self.arrived(self.fin.at[1 - c], self.cr)
        self.arrived(self.edges.at[1 - c], self.edge_recv)
        for copy in self.sent:
            copy.wait_send()


class StagedScatter(Scatter):
    def stage(self, buffers, sems, firsts):
        self.buffers, self.load_sems, self.firsts = buffers, sems, firsts

    def read(self, *refs):
        copies = [
            pltpu.make_async_copy(ref, self.buffers.at[i], self.load_sems.at[i]) for i, ref in enumerate(refs)
        ]
        for copy in copies:
            copy.start()
        for copy in copies:
            copy.wait()
        return [self.buffers[i].astype(F32) for i in range(len(refs))]

    def for_first(self, d):
        return self.firsts.at[d]

    def for_z(self, d):
        slot = self.firsts.at[d]
        copy = self.along_first.pop(d)
        copy.wait_send()
        self.sent = [e for e in self.sent if e is not copy]
        return slot


def scatter_scratch(outer, block):
    return [
        pltpu.VMEM((2 * outer,) + block, BF),
        pltpu.VMEM((outer,) + block, BF),
        pltpu.VMEM((max(outer - 1, 1),) + block, BF),
    ]


def scatter_sems(outer):
    return [
        DMA((2 * outer,)),
        DMA((2 * outer,)),
        DMA((outer,)),
        DMA((outer,)),
        DMA((outer,)),
        DMA((outer,)),
        DMA,
        DMA,
    ]


def dot(left, right, dims):
    return lax.dot_general(left, right, ((dims[0], dims[1]), ((), ())), preferred_element_type=F32)


NN = ((1,), (0,))
NT = ((1,), (1,))
TN = ((0,), (0,))


def spread(tail, rows, rem):
    extra = tail.shape[0]
    count = -(-rows // extra)
    return jnp.concatenate([tail[:, k * rem : (k + 1) * rem] for k in range(count)], 0)[:rows]


def squeezed(block, extra, main, column=None):
    parts = []
    for piece in (block,) if column is None else (block, column):
        rows, each = piece.shape
        count = -(-rows // extra)
        short = count * extra - rows
        if short:
            piece = jnp.concatenate([piece, jnp.zeros((short, each), piece.dtype)], 0)
        parts += [piece[k * extra : (k + 1) * extra] for k in range(count)]
    used = sum(p.shape[1] for p in parts)
    if used < main:
        parts.append(jnp.zeros((extra, main - used), block.dtype))
    return jnp.concatenate(parts, 1)


def store_rows(dst, src, main, rem):
    rows = src.shape[1] // 2
    for i in range(2):
        at = slice(i * rows, (i + 1) * rows)
        dst[i, 0:rows, :] = src[0:main, at].astype(F32).T.astype(dst.dtype)
        low = src[main : main + rem, at].astype(F32).T
        dst[i, rows:, :] = squeezed(low, dst.shape[1] - rows, main).astype(dst.dtype)


def store_packed(ref, index, value, main, rem):
    rows = value.shape[0]
    for h in range(2):
        at = ref.at[(h,) + index]
        at[0:rows, :] = value[:, h * main : (h + 1) * main].astype(ref.dtype)
        low = value[:, 2 * main + h * rem : 2 * main + (h + 1) * rem]
        at[rows:, :] = squeezed(low, at.shape[0] - rows, main).astype(ref.dtype)


def gelu_and_slope(u):
    share = 0.5 * (1.0 + lax.erf(u * 0.7071067811865476))
    return u * share, share + u * (jnp.exp(-0.5 * u * u) * 0.3989422804014327)


def mlp_kernel(
    wide, fc, rem, low2, cot_in, gm, residual, vec,
    pm, lo, grad_res, sums,
    weights, grads, tails, cot, low2_all, acc, got, wsem, rsend, rrecv, psem, xs, xr
):
    c, z, y, n, first, second = place()
    outer = wide // 2
    part = (outer + 1) // 2
    other = (1 - c, wide_of(z, y), n)
    beside = (c, wide_of(z, second[0]), second[1])
    rows, padded = low2.shape
    main = gm.shape[3]
    width = 2 * (main + rem)
    extra = gm.shape[2] - 2 * fc
    nf = wide * fc
    base = -(-2 * fc // extra) * rem
    greet([other, beside])
    mine, theirs = pl.ds(c * rows, rows), pl.ds((1 - c) * rows, rows)
    swap_low = remote(low2, low2_all.at[mine], xs.at[0], xr.at[0], other)
    swap_low.start()
    spots = [(y, n), first, second, (1 - y, 1 - n)]

    def pieces(d, spot):
        src = gm.at[wide_of(lax.rem(z + outer - d, outer), spot[0]), spot[1]]
        lanes = pl.ds(pl.multiple_of(spot[1] * main, LANES), main)
        out = []
        for k in range(2):
            at = pl.ds(pl.multiple_of((2 * d + spot[0]) * fc, 16), fc)
            out.append((src.at[pl.ds(k * fc, fc)], weights.at[k, at, lanes]))
        return out + [(src.at[pl.ds(2 * fc, extra)], tails.at[2 * d + spot[0], spot[1]])]

    def local(d):
        return [
            pltpu.make_async_copy(src, dst, wsem.at[d, i, k])
            for i, spot in enumerate(spots if d < part else spots[:2])
            for k, (src, dst) in enumerate(pieces(d, spot))
        ]

    def afar(d):
        return [
            remote(src, dst, rsend.at[d - part, i, k], rrecv.at[d - part, i, k], beside)
            for i, spot in enumerate(spots[:2])
            for k, (src, dst) in enumerate(pieces(d, spot))
        ]

    def landed(d):
        for i, spot in enumerate(spots[2:]):
            for k, (_, dst) in enumerate(pieces(d, spot)):
                remote(dst, dst, rrecv.at[d - part, i, k], rrecv.at[d - part, i, k], other).wait_recv()

    for d in range(part, outer):
        for copy in afar(d):
            copy.start()
    for d in range(outer):
        for copy in local(d):
            copy.start()

    low2_all[mine] = low2[...]
    for k in range(2):
        span = slice(k * rows, (k + 1) * rows)
        for h in range(2):
            cot[span, h * main : (h + 1) * main] = cot_in[k, h, 0:rows, :]
        cot[span, 2 * main :] = edge_tile([cot_in[k, h, rows:, :] for h in range(2)], rows, rem)

    def ready(begin, end):
        for d in range(begin, end):
            for copy in local(d):
                copy.wait()
            if d >= part:
                landed(d)
        for i in range(2 * begin, 2 * end):
            both = edge_tile([tails[i, h] for h in range(2)], 2 * fc, rem, base)
            for k in range(2):
                weights[k, i * fc : (i + 1) * fc, 2 * main :] = both[k * fc : (k + 1) * fc]

    ready(0, part)
    done = 2 * part * fc // 256 * 256
    acc[...] = jnp.zeros_like(acc)
    swap_low.wait_recv()

    def step(start, size):
        at = pl.ds(start, size)
        before = dot(low2_all[...], weights[0, at, :], NT)
        hidden, slope = gelu_and_slope(before)
        hidden = hidden.astype(BF)
        acc[0] += dot(hidden, weights[1, at, :], NN)
        grads[1, at, :] = dot(hidden, cot[...], TN).astype(BF)
        grad = dot(cot[...], weights[1, at, :], NT) * slope
        grad = grad.astype(BF)
        acc[1] += dot(grad, weights[0, at, :], NN)
        grads[0, at, :] = dot(grad, low2_all[...], TN).astype(BF)

    size = 256

    def steps(begin, end):
        full = (end - begin) // size

        @pl.loop(0, full)
        def _(j):
            step(pl.multiple_of(begin + j * size, size), size)

        if (end - begin) % size:
            step(begin + full * size, (end - begin) % size)

    steps(0, done)
    for d in range(part, outer):
        ready(d, d + 1)
        reach = nf if d == outer - 1 else 2 * (d + 1) * fc // size * size
        steps(done, reach)
        done = reach

    swap_acc = remote(acc.at[:, theirs], got, xs.at[1], xr.at[1], other)
    swap_acc.start()

    def grad_copies(i):
        dst = pm.at[wide_of(lax.rem(z + outer - i // 2, outer), i % 2)]
        out = []
        for h in range(2):
            for k in range(2):
                src = grads.at[k, i * fc : (i + 1) * fc, h * main : (h + 1) * main]
                out.append(pltpu.make_async_copy(src, dst.at[h, pl.ds(k * fc, fc)], psem.at[i, h, k]))
            out.append(pltpu.make_async_copy(tails.at[i, h], dst.at[h, pl.ds(2 * fc, extra)], psem.at[i, h, 2]))
        return out

    for i in range(wide):
        low = jnp.concatenate([grads[k, i * fc : (i + 1) * fc, 2 * main :] for k in range(2)], 0).astype(F32)
        for h in range(2):
            tails[i, h] = squeezed(
                low[:, h * rem : (h + 1) * rem], extra, main, low[:, 2 * rem : 2 * rem + 1]
            ).astype(BF)
        for copy in grad_copies(i):
            copy.start()

    swap_acc.wait_recv()
    result = residual[...] + (acc[0, mine] + got[0]) + vec[5:6]
    for h in range(2):
        lo[h, 0:main, :] = result[:, h * main : (h + 1) * main].T.astype(BF)
    edge = result[:, 2 * main :].T
    for h in range(2):
        lo[h, main:, :] = edge[h * rem : (h + 1) * rem].astype(BF)
    normed2, scale2 = normed_rows(residual[...], width)
    grad_low2 = acc[1, mine] + got[1]
    grad_out = cot[mine].astype(F32)
    lane = lax.broadcasted_iota(jnp.int32, grad_out.shape, 1)
    total = jnp.where(lane < width, grad_out + norm_back(grad_low2, normed2, scale2, vec[3:4], width), 0.0)
    grad_res[...] = total
    sums[...] = jnp.zeros_like(sums)
    sums[2:3] = jnp.sum(total.astype(BF).astype(F32), 0, keepdims=True)
    sums[3:4] = jnp.sum(grad_low2 * normed2, 0, keepdims=True)
    sums[4:5] = jnp.sum(grad_low2, 0, keepdims=True)
    sums[5:6] = jnp.sum(grad_out, 0, keepdims=True)

    for i in range(wide):
        for copy in grad_copies(i):
            copy.wait()
    for d in range(part, outer):
        for copy in afar(d):
            copy.wait_send()
    swap_low.wait_send()
    swap_acc.wait_send()


def mlp(low2, cot_in, gm, residual, vec, fc, rem):
    wide = gm.shape[0]
    rows, padded = low2.shape
    nf = wide * fc
    main = gm.shape[3]
    extra = gm.shape[2] - 2 * fc
    vmem = pl.BlockSpec(memory_space=pltpu.VMEM)
    return pl.pallas_call(
        functools.partial(mlp_kernel, wide, fc, rem),
        out_shape=(
            jax.ShapeDtypeStruct(gm.shape, BF),
            jax.ShapeDtypeStruct((2, main + rem, rows), BF),
            jax.ShapeDtypeStruct((rows, padded), F32),
            jax.ShapeDtypeStruct((16, padded), F32),
        ),
        in_specs=[vmem, vmem, ANY, vmem, vmem],
        out_specs=(ANY, vmem, vmem, vmem),
        scratch_shapes=[
            pltpu.VMEM((2, nf, padded), BF),
            pltpu.VMEM((2, nf, padded), BF),
            pltpu.VMEM((wide, 2, extra, main), BF),
            pltpu.VMEM((2 * rows, padded), BF),
            pltpu.VMEM((2 * rows, padded), BF),
            pltpu.VMEM((2, 2 * rows, padded), F32),
            pltpu.VMEM((2, rows, padded), F32),
            DMA((wide // 2, 4, 3)),
            DMA((wide // 2, 2, 3)),
            DMA((wide // 2, 2, 3)),
            DMA((wide, 2, 3)),
            DMA((2,)),
            DMA((2,)),
        ],
        compiler_params=pltpu.CompilerParams(
            collective_id=2, has_side_effects=True, vmem_limit_bytes=LIMIT
        ),
    )(low2, cot_in, gm, residual, vec)


def fill_mask(q_seg, k_seg, mask):
    keys, queries = mask.shape
    key = lax.broadcasted_iota(jnp.int32, (keys, queries), 0)
    query = lax.broadcasted_iota(jnp.int32, (keys, queries), 1) + (keys - queries)
    allowed = (k_seg[...] == q_seg[...]) & (key <= query)
    mask[...] = jnp.where(allowed, 0.0, NEGATIVE)


def turned(block):
    return block.astype(F32).T


def attend_pair(q, k, v, mask):
    q_t = turned(q) * SCALE
    row = lax.broadcasted_iota(jnp.int32, q_t.shape, 0)
    parts, logs = [], []
    for h in range(2):
        mine = (row >= h * HEAD) & (row < (h + 1) * HEAD)
        s = dot(k, jnp.where(mine, q_t, 0.0).astype(BF), NN) + mask[...]
        top = jnp.max(s, 0, keepdims=True)
        p = jnp.exp(s - top)
        total = jnp.sum(p, 0, keepdims=True)
        p = (p * (1.0 / total)).astype(BF)
        parts.append(dot(v, p, TN)[h * HEAD : (h + 1) * HEAD])
        logs.append(top + jnp.log(total))
    return jnp.concatenate(parts, 0).T.astype(BF), logs


def normed_rows(values, width):
    lane = lax.broadcasted_iota(jnp.int32, values.shape, 1)
    mean = jnp.sum(values, 1, keepdims=True) * (1.0 / width)
    centred = jnp.where(lane < width, values - mean, 0.0)
    scale = lax.rsqrt(jnp.sum(centred * centred, 1, keepdims=True) * (1.0 / width) + EPS)
    return centred * scale, scale


def norm_back(grad, normed, scale, gain, width):
    lane = lax.broadcasted_iota(jnp.int32, grad.shape, 1)
    scaled = jnp.where(lane < width, grad * gain, 0.0)
    first = jnp.sum(scaled, 1, keepdims=True) * (1.0 / width)
    second = jnp.sum(scaled * normed, 1, keepdims=True) * (1.0 / width)
    return scale * (scaled - first - normed * second)


def edge_tile(tails, rows, rem, base=None):
    tails = [t.astype(F32) for t in tails]
    parts = [spread(t, rows, rem) for t in tails]
    used = 2 * rem
    if base is not None:
        parts.append(spread(tails[0][:, base:], rows, 1))
        used += 1
    parts.append(jnp.zeros((rows, LANES - used), F32))
    return jnp.concatenate(parts, 1).astype(BF)


def forward_kernel(
    outer, hc, rem, x_in, cot_in, sa, sm, q_seg, k_seg, v0, v1, v2, v3, v4, v5,
    cot_out, gm, wa_out, x_out, low1_out, k_out, v_out, q, mixed, lse, residual, low2, vec,
    xin, cot, lines, ga, xs6, wa, x5, low1, k, v, mask, xs, xr, hs, hr, ks, kr, ls, os, *sems
):
    c, z, y, n, first, second = place()
    me = wide_of(z, y)
    wide = 2 * outer
    for src, dst in ((x_in, xin), (cot_in, cot)):
        store_rows(dst, src, sa.shape[1], rem)
    lines[...] = jnp.zeros_like(lines)
    for i, line in enumerate((v0, v1, v2, v3, v4, v5)):
        lines[n, i : i + 1, :] = line[...].astype(F32).reshape(1, -1)
    greet(partners(outer))
    other_n = (c, me, 1 - n)
    other_y = (c, wide_of(z, 1 - y), n)
    other_c = (1 - c, me, n)
    later = (c, wide_of(lax.rem(z + 1, outer), y), n)
    main = sa.shape[1]
    width = 2 * (main + rem)
    rows = q.shape[0]
    span = x5.shape[0]
    cols = 2 * hc
    sent = []

    def go(copy):
        copy.start()
        sent.append(copy)

    def arrived(dst, recv):
        remote(dst, dst, recv, recv, other_c).wait_recv()

    def x_send(j):
        src = xs6.at[n, j + 1 - n] if j < 4 else xin.at[1 - n]
        go(remote(src, xs6.at[n, j + 1 - n], hs.at[j], hr.at[j], other_n))

    own = xs6.at[n, pl.ds(4, 2)]
    keep = pltpu.make_async_copy(xin, own, ls.at[0])
    keep.start()
    keep_cot = pltpu.make_async_copy(cot.at[n], cot_out.at[c, n], ls.at[1])
    keep_cot.start()
    go(remote(lines.at[n], lines.at[n], xs.at[2], xr.at[2], other_n))
    go(remote(xin, xs6.at[n, pl.ds(0, 2)], xs.at[0], xr.at[0], later))
    x_send(4)
    heads = Gather(outer, sa, ga, True, (y, 1 - n), (1 - y, n), sems[:9])
    heads.start()
    heads.start_rest()
    fill_mask(q_seg, k_seg, mask)
    wa[:, width:, :] = jnp.zeros((4, wa.shape[1] - width, wa.shape[2]), BF)
    arrived(xs6.at[n, pl.ds(0, 2)], xr.at[0])
    keep.wait()
    x_send(0)
    go(remote(xs6.at[n, pl.ds(4 * (1 - y), 2)], xs6.at[n, pl.ds(2, 2)], xs.at[1], xr.at[1], other_y))
    for d in range(1, outer):
        heads.along_z(d)
    feed = Gather(outer, sm, gm, False, first, second, sems[9:], (outer + 1) // 2)
    feed.start()
    arrived(xs6.at[n, pl.ds(2, 2)], xr.at[1])
    for j in (1, 2, 3):
        x_send(j)
    for d in range(outer):
        heads.along_first(d)
    go(remote(cot.at[1 - n], cot_out.at[c, n], ks.at[0], kr.at[0], other_n))
    go(remote(cot.at[n], cot_out.at[c, n], ks.at[1], kr.at[1], other_c))
    feed.start_rest()

    arrived(lines.at[1 - n], xr.at[2])
    row = lax.broadcasted_iota(jnp.int32, (8, LANES), 0)
    lane = lax.broadcasted_iota(jnp.int32, (8, LANES), 1)
    unit = jnp.where(((row == 1) | (row == 4)) & (lane == 2 * rem), 1.0, 0.0)
    vec[...] = jnp.zeros_like(vec)
    for h in range(2):
        vec[0:8, h * main : (h + 1) * main] = lines[h, :, 0:main]
    edges = [lines[h, :, main:] for h in range(2)]
    vec[0:8, 2 * main :] = unit + jnp.concatenate(edges + [jnp.zeros((8, LANES - 2 * rem), F32)], 1)
    for j in range(5):
        arrived(xs6.at[1 - n, j + n], hr.at[j])
    for j in range(5):
        at = slice(j * rows, (j + 1) * rows)
        for h in range(2):
            x5[at, h * main : (h + 1) * main] = xs6[h, n + j, 0:rows, :]
        x5[at, 2 * main :] = edge_tile([xs6[h, n + j, rows:, :] for h in range(2)], rows, rem)
    outs = [pltpu.make_async_copy(x5, x_out, os.at[0])]
    outs[0].start()
    for kk in range(2):
        for d in range(outer):
            heads.along_second(d, kk)
    heads.finish()

    block_rows = up16(4 * hc)
    extra = ga.shape[3] - block_rows
    base = -(-block_rows // extra) * rem
    for i in range(wide):
        for half in range(2):
            edge = edge_tile([ga[half, i, h, block_rows:, :] for h in range(2)], block_rows, rem, base)
            for s in range(4):
                src = slice(s * hc, (s + 1) * hc)
                to = slice(i * cols + half * hc, i * cols + (half + 1) * hc)
                for h in range(2):
                    wa[s, to, h * main : (h + 1) * main] = ga[half, i, h, src, :]
                wa[s, to, 2 * main :] = edge[src]
    outs.append(pltpu.make_async_copy(wa, wa_out, os.at[1]))
    outs[1].start()
    feed.along_z(1)

    @pl.loop(0, span // rows)
    def _(j):
        at = pl.ds(pl.multiple_of(j * rows, rows), rows)
        normed, _ = normed_rows(x5[at, :].astype(F32), width)
        low1[at, :] = (normed * vec[0:1] + vec[1:2]).astype(BF)
        k[at, :] = dot(low1[at, :], wa[1], NT).astype(BF)
        v[at, :] = dot(low1[at, :], wa[2], NT).astype(BF)

    q[...] = dot(low1[span - rows :, :], wa[0], NT).astype(BF)
    for src, dst in ((low1, low1_out), (k, k_out), (v, v_out)):
        outs.append(pltpu.make_async_copy(src, dst, os.at[len(outs)]))
        outs[-1].start()

    pairs = q.shape[1] // LANES
    lse[...] = jnp.zeros_like(lse)

    def some(begin, end):
        @pl.loop(begin, end)
        def _(i):
            at = pl.ds(pl.multiple_of(i * LANES, LANES), LANES)
            out, logs = attend_pair(q[:, at], k[:, at], v[:, at], mask)
            mixed[:, at] = out
            for h in range(2):
                lse[i, pl.ds(h, 1), :] = logs[h]

    for d in range(2, outer):
        feed.along_z(d)
    cuts = [0, pairs // 3, 2 * pairs // 3, pairs]
    some(cuts[0], cuts[1])
    for d in range(feed.part):
        feed.along_first(d)
    arrived(cot_out.at[c, 1 - n], kr.at[0])
    go(remote(cot_out.at[c, 1 - n], cot_out.at[c, 1 - n], ks.at[2], kr.at[2], other_c))
    some(cuts[1], cuts[2])
    some(cuts[2], cuts[3])
    value = x5[span - rows :, :].astype(F32) + dot(mixed[...], wa[3], NN) + vec[2:3]
    residual[...] = value
    normed, _ = normed_rows(value, width)
    low2[...] = (normed * vec[3:4] + vec[4:5]).astype(BF)

    for d in range(feed.part, outer):
        feed.along_first(d)
    for kk in range(2):
        for d in range(outer):
            feed.along_second(d, kk)
    arrived(cot_out.at[1 - c, n], kr.at[1])
    arrived(cot_out.at[1 - c, 1 - n], kr.at[2])
    keep_cot.wait()
    for copy in outs:
        copy.wait()
    for copy in sent:
        copy.wait_send()
    feed.finish()


def forward(x_in, cot_in, sa, sm, q_seg, k_seg, vectors, hc, rem):
    wide = lax.axis_size("wide")
    outer = wide // 2
    main = sa.shape[1]
    width = 2 * (main + rem)
    padded = -(-(width + 1) // LANES) * LANES
    rows = q_seg.shape[1]
    span = k_seg.shape[0]
    block = (2, rows + rem_rows(rows, main + rem), main)
    pairs = padded // LANES
    vmem = pl.BlockSpec(memory_space=pltpu.VMEM)
    shape = jax.ShapeDtypeStruct
    return pl.pallas_call(
        functools.partial(forward_kernel, outer, hc, rem),
        out_shape=(
            shape((2,) + block, BF),
            shape((wide, 2) + sm.shape, BF),
            shape((4, padded, padded), BF),
            shape((span, padded), BF),
            shape((span, padded), BF),
            shape((span, padded), BF),
            shape((span, padded), BF),
            shape((rows, padded), BF),
            shape((rows, padded), BF),
            shape((pairs, 8, rows), F32),
            shape((rows, padded), F32),
            shape((rows, padded), BF),
            shape((16, padded), F32),
        ),
        in_specs=[vmem] * 2 + [ANY] * 2 + [vmem] * (2 + len(vectors)),
        out_specs=(ANY,) * 7 + (vmem,) * 6,
        scratch_shapes=[
            pltpu.VMEM(block, BF),
            pltpu.VMEM(block, BF),
            pltpu.VMEM((2, 8, main + rem), F32),
            pltpu.VMEM((2, wide, 2) + sa.shape, BF),
            pltpu.VMEM((2, 6) + block[1:], BF),
            pltpu.VMEM((4, padded, padded), BF),
            pltpu.VMEM((span, padded), BF),
            pltpu.VMEM((span, padded), BF),
            pltpu.VMEM((span, padded), BF),
            pltpu.VMEM((span, padded), BF),
            pltpu.VMEM((span, rows), F32),
        ]
        + [DMA((3,)), DMA((3,)), DMA((5,)), DMA((5,)), DMA((3,)), DMA((3,)), DMA((2,)), DMA((5,))]
        + gather_sems(outer)
        + gather_sems(outer),
        compiler_params=pltpu.CompilerParams(
            collective_id=0, has_side_effects=True, vmem_limit_bytes=LIMIT
        ),
    )(x_in, cot_in, sa, sm, q_seg, k_seg, *vectors)


def attend_back_pair(q, k, v, g, lse, mask):
    q_n = q.astype(F32) * SCALE
    g_n = g.astype(F32)
    q_t, g_t = q_n.T, g_n.T
    row = lax.broadcasted_iota(jnp.int32, q_t.shape, 0)
    lane = lax.broadcasted_iota(jnp.int32, q_n.shape, 1)
    parts = []
    dk_sum = dv_sum = None
    for h in range(2):
        in_row = (row >= h * HEAD) & (row < (h + 1) * HEAD)
        in_lane = (lane >= h * HEAD) & (lane < (h + 1) * HEAD)
        s = dot(k, jnp.where(in_row, q_t, 0.0).astype(BF), NN) + mask[...]
        p = jnp.exp(s - lse[h : h + 1])
        dp = dot(v, jnp.where(in_row, g_t, 0.0).astype(BF), NN)
        delta = jnp.sum(p * dp, 0, keepdims=True)
        ds = (p * (dp - delta)).astype(BF)
        one = dot(ds, jnp.where(in_lane, q_n, 0.0).astype(BF), NN)
        two = dot(p.astype(BF), jnp.where(in_lane, g_n, 0.0).astype(BF), NN)
        dk_sum = one if dk_sum is None else dk_sum + one
        dv_sum = two if dv_sum is None else dv_sum + two
        parts.append(dot(k, ds, TN)[h * HEAD : (h + 1) * HEAD] * SCALE)
    return jnp.concatenate(parts, 0).T.astype(BF), dk_sum.astype(BF), dv_sum.astype(BF)


def backward_kernel(
    outer, hc, rem, grad_res, q, lse, q_seg, k_seg, vec, sums_in, k_in, v_in, wa_in, x_in, low1_in, mixed_in, pm, lo,
    mo, ao, em, ea, xg, vec_out, lo_out, m1, m2, m3, pcore,
    pool, k, v, dk, dv, dq, g, branch, mask, stage, firsts, a1, a2, a3, pa, po, edge,
    pg, got_x, got_y, got_z, out_y, out_z, sums, vx, vz,
    ls, xs, xr, hs, hr, cs, cr, vs, vr, ps, ms, es, *sems
):
    c, z, y, n, first, second = place()
    me = wide_of(z, y)
    wide = 2 * outer
    greet(partners(outer))
    other_n = (c, me, 1 - n)
    other_y = (c, wide_of(z, 1 - y), n)
    other_c = (1 - c, me, n)
    earlier = (c, wide_of(lax.rem(z + outer - 1, outer), y), n)
    main = pm.shape[3]
    width = 2 * (main + rem)
    rows, padded = q.shape
    span = k.shape[0]
    blocks = span // rows
    cols = 2 * hc
    block_rows = edge.shape[0]
    extra = pa.shape[2] - block_rows
    sent = []

    def go(copy):
        copy.start()
        sent.append(copy)

    def arrived(dst, recv):
        remote(dst, dst, recv, recv, other_c).wait_recv()

    feed = StagedScatter(
        outer, first, second, lambda z, y, n: pm.at[wide_of(z, y), n], m1, m2, m3, mo, sems[:8]
    )
    feed.stage(stage, ms, firsts)
    loads = [
        pltpu.make_async_copy(src, dst, ls.at[i])
        for i, (src, dst) in enumerate(
            (
                (wa_in.at[3], pool.at[0]),
                (k_in, k),
                (v_in, v),
                (wa_in.at[1], pool.at[1]),
                (wa_in.at[2], pool.at[2]),
                (wa_in.at[0], pool.at[0]),
                (x_in, v),
                (low1_in, k),
                (mixed_in, g),
                (lo.at[n], lo_out.at[:, pl.ds(pl.multiple_of(n * rows, LANES), rows)]),
            )
        )
    ]
    for copy in loads[:5] + loads[9:]:
        copy.start()
    feed.start()
    mine = lo_out.at[:, pl.ds(pl.multiple_of(n * rows, LANES), rows)]
    go(remote(lo.at[1 - n], mine, xs.at[2], xr.at[2], other_n))
    fill_mask(q_seg, k_seg, mask)
    branch[...] = grad_res[...].astype(BF)
    loads[0].wait()
    g[...] = dot(branch[...], pool[0], NT).astype(BF)
    loads[5].start()
    loads[1].wait()
    loads[2].wait()
    pairs = padded // LANES

    def some(begin, end):
        @pl.loop(begin, end)
        def _(i):
            at = pl.ds(pl.multiple_of(i * LANES, LANES), LANES)
            one, two, three = attend_back_pair(q[:, at], k[:, at], v[:, at], g[:, at], lse[i], mask)
            dq[:, at] = one
            dk[:, at] = two
            dv[:, at] = three

    steps = feed.steps()

    def pump(count):
        for _ in range(min(count, len(steps))):
            steps.pop(0)()

    some(0, pairs // 2)
    pump(1)
    some(pairs // 2, pairs)
    for copy in loads[6:9]:
        copy.start()
    sums[...] = sums_in[...]
    for copy in loads[3:7]:
        copy.wait()

    def input_part(j, extra_part):
        at = pl.ds(j * rows, rows)
        grad = dot(dk[at, :], pool[1], NN) + dot(dv[at, :], pool[2], NN)
        if extra_part:
            grad = grad + dot(dq[...], pool[0], NN)
        normed, scale = normed_rows(v[at, :].astype(F32), width)
        sums[0:1] += jnp.sum(grad * normed, 0, keepdims=True)
        sums[1:2] += jnp.sum(grad, 0, keepdims=True)
        back = norm_back(grad, normed, scale, vec[0:1], width)
        if extra_part:
            back = back + grad_res[...]
        store_packed(pg, (j,), back, main, rem)

    def x_back(j):
        go(remote(pg.at[1 - n, j], got_x.at[j], hs.at[j], hr.at[j], other_n))

    for j in (2, 1, 3, 0):
        input_part(j, False)
        x_back(j)
        if j == 1:
            pump(1)
    input_part(blocks - 1, True)
    x_back(blocks - 1)
    vx[0] = sums[...]
    go(remote(vx.at[0], vx.at[1], vs.at[0], vr.at[0], other_c))

    def products(s, left, right):
        size = 256
        for begin in range(0, padded, size):
            stop = min(begin + size, padded)
            pool[s, begin:stop, :] = dot(left[:, begin:stop], right, TN).astype(BF)

    for copy in loads[7:9]:
        copy.wait()
    products(3, g, branch[...])
    pump(1)
    products(0, dq, k[span - rows :, :])
    arrived(vx.at[1], vr.at[0])
    vz[z] = vx[0] + vx[1]
    for d in range(1, outer):
        device = (c, wide_of(lax.rem(z + d, outer), y), n)
        go(remote(vz.at[z], vz.at[z], vs.at[2 + d], vr.at[2 + d], device))
    products(1, dk, k[...])
    pump(2)
    products(2, dv, k[...])
    pump(1)

    def place_rows(i, core, out):
        for s in range(4):
            to = slice(s * hc, (s + 1) * hc)
            src = slice(i * cols + core * hc, i * cols + (core + 1) * hc)
            for h in range(2):
                out[h, to, :] = pool[s, src, h * main : (h + 1) * main]
            edge[to, :] = pool[s, src, 2 * main :]
        if block_rows > 4 * hc:
            gap = slice(4 * hc, block_rows)
            for h in range(2):
                out[h, gap, :] = jnp.zeros((block_rows - 4 * hc, main), BF)
            edge[gap, :] = jnp.zeros((block_rows - 4 * hc, LANES), BF)
        low = edge[...].astype(F32)
        for h in range(2):
            out[h, block_rows:, :] = squeezed(
                low[:, h * rem : (h + 1) * rem], extra, main, low[:, 2 * rem : 2 * rem + 1]
            ).astype(BF)

    def to_core(i):
        return remote(po.at[i % 2], pcore.at[i], cs.at[i], cr.at[i], other_c)

    for i in range(wide):
        if i >= 2:
            to_core(i - 2).wait_send()
        for core in range(2):
            pl.when(c == core)(functools.partial(place_rows, i, 1 - core, po.at[i % 2]))
        to_core(i).start()

    for i in range(wide):
        for core in range(2):
            pl.when(c == core)(functools.partial(place_rows, i, core, pa.at[i]))
    def fetch(i):
        arrived(pcore.at[i], cr.at[i])
        copy = pltpu.make_async_copy(pcore.at[i], po.at[i % 2], ps.at[i % 2])
        copy.start()
        return copy

    for i in range(max(wide - 2, 0), wide):
        to_core(i).wait_send()
    copies = [fetch(0)]
    for i in range(wide):
        if i + 1 < wide:
            copies.append(fetch(i + 1))
        copies[i].wait()
        for h in range(2):
            pa[i, h] = (pa[i, h].astype(F32) + po[i % 2, h].astype(F32)).astype(BF)
    heads = Scatter(
        outer, first, second, lambda z, y, n: pa.at[wide_of(z, y), n], a1, a2, a3, ao, sems[8:]
    )
    heads.start(0, 1)
    pump(len(steps))
    late = heads.steps()
    for d in range(1, outer):
        arrived(vz.at[lax.rem(z + outer - d, outer)], vr.at[2 + d])
    total = vz[0]
    for i in range(1, outer):
        total = total + vz[i]
    vx[2] = total
    go(remote(vx.at[2], vx.at[3], vs.at[1], vr.at[1], other_y))

    def summed(b):
        if b == 0:
            return jnp.where(n == 0, pg[n, 0].astype(F32), got_x[0].astype(F32))
        if b == 5:
            return jnp.where(n == 1, pg[n, 4].astype(F32), got_x[4].astype(F32))
        return pg[n, b - n].astype(F32) + got_x[b - 1 + n].astype(F32)

    for j in (2, 1, 3):
        arrived(got_x.at[j], hr.at[j])
    for b in range(2):
        out_y[b] = summed(2 + b).astype(BF)
    go(remote(out_y, got_y, xs.at[0], xr.at[0], other_y))
    heads.start(1)
    late.pop(0)()
    arrived(vx.at[3], vr.at[1])
    vx[4] = vx[2] + vx[3]
    go(remote(vx.at[4], vx.at[5], vs.at[2], vr.at[2], other_n))
    for j in (0, 4):
        arrived(got_x.at[j], hr.at[j])
    arrived(got_y, xr.at[0])
    for b in range(2):
        out_z[b] = (summed(b) + jnp.where(y == 1, got_y[b].astype(F32), 0.0)).astype(BF)
    go(remote(out_z, got_z, xs.at[1], xr.at[1], earlier))
    for _ in range(min(2, len(late))):
        late.pop(0)()
    feed.close(em, rem, es.at[0])
    for step in late:
        step()
    arrived(got_z, xr.at[1])
    for b in range(2):
        value = summed(4 + b) + jnp.where(y == 0, got_y[b].astype(F32), 0.0)
        value = value + got_z[b].astype(F32)
        at = slice(b * rows, (b + 1) * rows)
        xg[0:main, at] = value[0:rows].T.astype(BF)
        edge_x = jnp.concatenate([spread(value[rows:], rows, rem), jnp.zeros((rows, LANES - rem), F32)], 1)
        xg[main:, at] = edge_x.T[0:rem].astype(BF)
    arrived(vx.at[5], vr.at[2])
    total = vx[4] + vx[5]
    vec_out[:, 0:main] = jnp.where(n == 0, total[:, 0:main], total[:, main : 2 * main])
    edge_a, edge_b = total[:, 2 * main : 2 * main + rem], total[:, 2 * main + rem : 2 * main + 2 * rem]
    vec_out[:, main:] = jnp.where(n == 0, edge_a, edge_b)
    heads.close(ea, rem, es.at[1])
    loads[9].wait()
    arrived(lo_out.at[:, pl.ds(pl.multiple_of((1 - n) * rows, LANES), rows)], xr.at[2])
    for copy in sent:
        copy.wait_send()
    feed.finish()
    heads.finish()


def backward(grad_res, q, lse, q_seg, k_seg, vec, sums, k, v, wa, x5, low1, mixed, pm, lo, hc, fc2, rem):
    wide = pm.shape[0]
    outer = wide // 2
    rows, padded = q.shape
    span = k.shape[0]
    main = pm.shape[3]
    half = main + rem
    bm, bx = pm.shape[2:], (rows + rem_rows(rows, half), main)
    block_rows = up16(4 * hc)
    ba = (block_rows + rem_rows(block_rows, main + rem), main)
    vmem = pl.BlockSpec(memory_space=pltpu.VMEM)
    shape = jax.ShapeDtypeStruct
    few = max(outer - 1, 1)
    return pl.pallas_call(
        functools.partial(backward_kernel, outer, hc, rem),
        out_shape=(
            shape((2,) + bm, F32),
            shape((2,) + ba, F32),
            shape((2, fc2, LANES), F32),
            shape((2, block_rows, LANES), F32),
            shape((half, 2 * rows), BF),
            shape((sums.shape[0], half), F32),
            shape((half, 2 * rows), BF),
            shape((2 * outer,) + bm, BF),
            shape((outer,) + bm, BF),
            shape((few,) + bm, BF),
            shape((wide, 2) + ba, BF),
        ),
        in_specs=[vmem] * 7 + [ANY] * 8,
        out_specs=(vmem,) * 6 + (ANY,) * 5,
        scratch_shapes=[
            pltpu.VMEM((4, padded, padded), BF),
            pltpu.VMEM((span, padded), BF),
            pltpu.VMEM((span, padded), BF),
            pltpu.VMEM((span, padded), BF),
            pltpu.VMEM((span, padded), BF),
            pltpu.VMEM((rows, padded), BF),
            pltpu.VMEM((rows, padded), BF),
            pltpu.VMEM((rows, padded), BF),
            pltpu.VMEM((span, rows), F32),
            pltpu.VMEM((3,) + bm, BF),
            pltpu.VMEM((outer,) + bm, BF),
        ]
        + scatter_scratch(outer, ba)
        + [
            pltpu.VMEM((wide, 2) + ba, BF),
            pltpu.VMEM((2, 2) + ba, BF),
            pltpu.VMEM((block_rows, LANES), BF),
            pltpu.VMEM((2, span // rows) + bx, BF),
            pltpu.VMEM((5,) + bx, BF),
            pltpu.VMEM((2,) + bx, BF),
            pltpu.VMEM((2,) + bx, BF),
            pltpu.VMEM((2,) + bx, BF),
            pltpu.VMEM((2,) + bx, BF),
            pltpu.VMEM(sums.shape, F32),
            pltpu.VMEM((6,) + sums.shape, F32),
            pltpu.VMEM((outer,) + sums.shape, F32),
        ]
        + [DMA((10,)), DMA((3,)), DMA((3,)), DMA((5,)), DMA((5,)), DMA((wide,)), DMA((wide,))]
        + [DMA((2 + outer,)), DMA((2 + outer,)), DMA((2,)), DMA((3,)), DMA((2, 2))]
        + scatter_sems(outer)
        + scatter_sems(outer),
        compiler_params=pltpu.CompilerParams(
            collective_id=1, has_side_effects=True, vmem_limit_bytes=LIMIT
        ),
    )(grad_res, q, lse, q_seg, k_seg, vec, sums, k, v, wa, x5, low1, mixed, pm, lo)


def shards(
    layer_input,
    doc_segments,
    first_gain,
    first_shift,
    heads_weight,
    query_bias,
    value_bias,
    merge_weight,
    merge_bias,
    second_gain,
    second_shift,
    up_weight,
    up_bias,
    down_weight,
    down_bias,
    out_cotangent,
):
    parts = lax.axis_size("narrow")
    wide = lax.axis_size("wide")
    c, w, n = lax.axis_index("dp"), lax.axis_index("wide"), lax.axis_index("narrow")
    half = heads_weight.shape[0]
    width = half * parts
    padded = -(-width // LANES) * LANES
    cols = heads_weight.shape[2]
    units = up_weight.shape[1]
    hc, fc = cols // 2, up16(units // 2)
    short = fc - units // 2
    rows = layer_input.shape[0] // parts
    span = (REACH + 1) * rows

    by_half = heads_weight.transpose(1, 2, 0).reshape(3, 2, hc, half)
    heads_rows = lax.dynamic_index_in_dim(by_half, c, 1, False).reshape(3 * hc, half)
    merge_rows = lax.dynamic_slice_in_dim(merge_weight, c * hc, hc, 0)
    up_rows = lax.dynamic_slice_in_dim(up_weight, c * (units // 2), units // 2, 1).T
    down_rows = lax.dynamic_slice_in_dim(down_weight, c * (units // 2), units // 2, 0)
    up_rows = jnp.pad(up_rows, ((0, short), (0, 0)))
    down_rows = jnp.pad(down_rows, ((0, short), (0, 0)))
    line = lambda *v: jnp.pad(jnp.concatenate(v), (0, half - sum(e.shape[0] for e in v)))
    vectors = [first_gain, first_shift, merge_bias, second_gain, second_shift, down_bias]
    gap = up16(4 * hc) - 4 * hc
    sa = jnp.concatenate([heads_rows, merge_rows] + ([jnp.zeros((gap, half), BF)] if gap else []), 0)
    part = lambda v, size: lax.dynamic_slice_in_dim(v, c * size, size, 0)
    zero = lambda size: jnp.zeros((size,), BF)
    column_a = jnp.concatenate([part(query_bias, hc), zero(hc), part(value_bias, hc), zero(hc + gap)])
    sm = jnp.concatenate([up_rows, down_rows], 0)
    column_m = jnp.concatenate([part(up_bias, units // 2), zero(short + fc)])
    start = (w * parts + n) * rows
    ahead = jnp.pad(doc_segments, ((0, 0), (REACH * rows, 0)), constant_values=-1)
    segments = lax.dynamic_slice(ahead, (c, start), (1, span))
    k_seg = segments.reshape(span, 1)
    q_seg = segments[:, span - rows :]

    rem = widths(half)[1]
    cot_all, gm, wa, x5, low1, key, value, query, mixed, lse, residual, low2, vec = forward(
        layer_input.T, out_cotangent.T, pack(sa, column_a), pack(sm, column_m), q_seg, k_seg, vectors, hc, rem
    )
    pm, lo, grad_residual, sums = mlp(low2, cot_all, gm, residual, vec, fc, rem)

    mo, ao, em, ea, input_grad, lines, layer_output, _, _, _, _ = backward(
        grad_residual, query, lse, q_seg, k_seg, vec, sums, key, value, wa, x5, low1, mixed, pm, lo, hc, 2 * fc, rem
    )

    def total(block, edge, begin, size):
        at = slice(begin, begin + size)
        return jnp.concatenate([block[:, at], edge[:, at, :rem]], -1)

    input_grad, layer_output = input_grad.T, layer_output.T
    heads_total = total(ao, ea, 0, 3 * hc).reshape(2, 3, hc, half).transpose(3, 1, 0, 2).reshape(half, 3, cols)
    merge_total = total(ao, ea, 3 * hc, hc).reshape(cols, half)
    up_total = total(mo, em, 0, units // 2).reshape(units, half).T
    down_total = total(mo, em, fc, units // 2).reshape(units, half)
    up_bias_total = em[:, : units // 2, rem].reshape(units)
    query_total = ea[:, :hc, rem].reshape(cols)
    value_total = ea[:, 2 * hc : 3 * hc, rem].reshape(cols)
    return (
        layer_output,
        input_grad,
        lines[0],
        lines[1],
        heads_total,
        query_total,
        value_total,
        merge_total,
        lines[2],
        lines[3],
        lines[4],
        up_total,
        up_bias_total,
        down_total,
        lines[5],
    )


def solution(mesh):
    return jax.shard_map(
        shards,
        mesh=mesh,
        in_specs=(
            P(("dp", "wide"), "narrow"),
            P(),
            P("narrow"),
            P("narrow"),
            P("narrow", None, "wide"),
            P("wide"),
            P("wide"),
            P("wide", "narrow"),
            P("narrow"),
            P("narrow"),
            P("narrow"),
            P("narrow", "wide"),
            P("wide"),
            P("wide", "narrow"),
            P("narrow"),
            P(("dp", "wide"), "narrow"),
        ),
        out_specs=(
            P(("dp", "wide"), "narrow"),
            P(("dp", "wide"), "narrow"),
            P("narrow"),
            P("narrow"),
            P("narrow", None, "wide"),
            P("wide"),
            P("wide"),
            P("wide", "narrow"),
            P("narrow"),
            P("narrow"),
            P("narrow"),
            P("narrow", "wide"),
            P("wide"),
            P("wide", "narrow"),
            P("narrow"),
        ),
        check_vma=False,
    )
```

profile of v0, /device:TPU:11, one launch (start us, length us, event | category | flops | bytes accessed | tf_op | source)
XLA Modules:
  0.0 387.2 jit_solution(12077615834225648430)
XLA Ops:
  0.6 0.0 copy-start
  0.7 0.0 copy-start.7
  0.7 1.4 pad_dynamic-slice_fusion.q_seg
  2.1 0.7 dynamic_slice.27
  2.8 0.7 dynamic_slice.28
  3.6 0.1 fusion.15
  3.7 0.8 dynamic_slice.31
  4.4 0.1 reshape.80
  4.5 0.1 reshape.77
  4.6 0.1 copy.38
  4.7 0.8 fusion.8
  5.5 0.1 copy.41
  5.6 0.9 constant_dynamic-slice_fusion.2
  6.5 0.0 copy-done
  6.6 0.0 copy-done.7
  6.6 0.2 constant_dynamic-slice_fusion.1
  6.8 0.2 copy.47
  7.1 0.0 copy-start.6
  7.1 0.1 copy.50
  7.2 0.2 reshape.79
  7.4 0.1 slice.111
  7.5 0.9 maximum_maximum_fusion.sm
  8.4 0.0 copy-done.6
  8.4 0.1 reshape.73
  8.5 0.1 reshape.74
  8.7 0.1 copy.51
  8.7 0.2 reshape.76
  8.9 0.1 slice.107
  9.0 0.8 maximum_maximum_fusion.1.sa
  9.8 1.1 copy.42.k_seg
  10.9 135.3 %shard_map.271 = (bf16[2,2,272,512]{3,2,1,0:T(8,128)(2,1)}, bf16[8,2,592,512]{3,2,1,0:T(8,128)(2,1)}, bf16[4,1152,1152]{2,1,0:T(8,128)(2,1)}, bf16[1280,1152]{1,...) custom-call(bf16[544,512]{1,0:T(8,128)(2,1)} %bitcast.34, ...), custom_call_target="tpu_custom_call" | custom-call | tf_op jit(solution)/shard_map/pallas_call | solution.py:873
  146.1 51.1 %shard_map.272 = (bf16[8,2,592,512]{3,2,1,0:T(8,128)(2,1)}, bf16[2,544,256]{2,1,0:T(8,128)(2,1)}, f32[256,1152]{1,0:T(8,128)}, f32[16,1152]{1,0:T(8,128)}) custom-call(bf16[256,1152]{1,0:T(8,128)(2,1)} %get-tuple-element.39.low2, bf16[2,2,272,512]{3,2,1,0:T(8,128)(2,1)} %get-tuple-element.40.cot_in, bf16[8,2,592,512]{3,2,1,0:T(8,128)(2,1)} %get-tuple-element.41.gm, ...), custom_call_target="tpu_custom_call" | custom-call | tf_op jit(solution)/shard_map/pallas_call | solution.py:615
  197.3 172.8 %shard_map.273 = (f32[2,592,512]{2,1,0:T(8,128)}, f32[2,304,512]{2,1,0:T(8,128)}, f32[2,544,128]{2,1,0:T(8,128)}, f32[2,272,128]{2,1,0:T(8,128)}, bf16[544,512]{...) custom-call(f32[256,1152]{1,0:T(8,128)} %get-tuple-element.44.grad_r, ...), custom_call_target="tpu_custom_call" | custom-call | tf_op jit(solution)/shard_map/pallas_call | solution.py:1199
  370.1 0.0 copy-start.3
  370.1 0.0 copy-start.2
  370.1 1.3 slice_reduce_fusion.1
  371.4 0.6 reshape_squeeze.10
  372.1 0.6 reshape_squeeze.9
  372.7 1.2 slice_reduce_fusion
  373.9 1.1 fusion.17
  375.0 0.7 reshape_squeeze.11
  375.7 1.7 slice_reduce_fusion.3
  377.4 0.0 copy-done.3
  377.5 0.0 copy-done.2
  377.5 0.1 slice.89
  377.6 0.1 pad_maximum_fusion.2
  377.7 0.5 copy.44
  378.3 0.8 reshape.84
  379.0 0.1 copy.45
  379.1 1.1 reshape.83
  380.2 1.8 fusion.16
  381.9 1.3 pad_maximum_fusion
  383.3 0.0 copy-start.5
  383.3 0.0 copy-start.1
  383.3 1.6 copy.46
  384.8 0.0 copy-start.4
  384.8 0.0 copy-done.5
  384.8 0.8 copy.54
  385.6 0.4 copy-done.4
  386.1 0.8 copy.55
  386.9 0.0 copy-done.1
  (14 shorter events, 0.3 us)
Async XLA Ops:
  0.6 5.9 %copy-start = (bf16[544,544]{1,0:T(8,128)(2,1)S(1)}, bf16[544,544]{1,0:T(8,128)(2,1)}, u32[]{:S(2)}) copy-start(bf16[544,544]{1,0:T(8,128)(2,1)} %param.29) | copy-start | bytes 1775620
  0.7 5.9 %copy-start.7 = (bf16[544,544]{1,0:T(8,128)(2,1)S(1)}, bf16[544,544]{1,0:T(8,128)(2,1)}, u32[]{:S(2)}) copy-start(bf16[544,544]{1,0:T(8,128)(2,1)} %param.27) | copy-start | bytes 1775620
  7.1 1.3 copy-start.6
  370.1 7.3 %copy-start.3 = (f32[2,272,128]{2,1,0:T(8,128)S(1)}, f32[2,272,128]{2,1,0:T(8,128)}, u32[]{:S(2)}) copy-start(f32[2,272,128]{2,1,0:T(8,128)} %get-tuple-element.60) | copy-start | bytes 835588
  370.1 7.3 %copy-start.2 = (f32[2,304,512]{2,1,0:T(8,128)S(1)}, f32[2,304,512]{2,1,0:T(8,128)}, u32[]{:S(2)}) copy-start(f32[2,304,512]{2,1,0:T(8,128)} %get-tuple-element.59) | copy-start | bytes 3735556
  383.3 1.6 copy-start.5
  383.3 3.6 copy-start.1
  384.8 1.3 copy-start.4
where the time goes:
time: 393 us; the launch traced here: 387 us
  Pallas kernels  359 us (91%)
  local copies, waits for them, and re-layouts  23.4 us (6%)
    pallas_call x1, Pallas kernels, backward(): pl.pallas_call(functools.partial(backward_kernel, outer, hc, rem), out_sh...  173 us
    pallas_call x1, Pallas kernels, forward(): pl.pallas_call(functools.partial(forward_kernel, outer, hc, rem), out_sha...  135 us
    pallas_call x1, Pallas kernels, mlp(): pl.pallas_call(functools.partial(mlp_kernel, wide, fc, rem), out_shape=(j...  51.1 us

commit v1 on v0

--- a/solution.py
+++ b/solution.py
@@ -519,7 +519,8 @@
                 weights[k, i * fc : (i + 1) * fc, 2 * main :] = both[k * fc : (k + 1) * fc]
 
     ready(0, part)
-    done = 2 * part * fc // 256 * 256
+    size = 512
+    done = 2 * part * fc // size * size
     acc[...] = jnp.zeros_like(acc)
     swap_low.wait_recv()
 
@@ -535,7 +536,6 @@
         acc[1] += dot(grad, weights[0, at, :], NN)
         grads[0, at, :] = dot(grad, low2_all[...], TN).astype(BF)
 
-    size = 256
 
     def steps(begin, end):
         full = (end - begin) // size

time: 393 us -> 389 us (0.990)
  no operation moved by 1% of the time
where the time goes in v1:
time: 389 us; the launch traced here: 384 us
  Pallas kernels  356 us (92%)
  local copies, waits for them, and re-layouts  23.4 us (6%)
    pallas_call x1, Pallas kernels, backward(): pl.pallas_call(functools.partial(backward_kernel, outer, hc, rem), out_sh...  173 us
    pallas_call x1, Pallas kernels, forward(): pl.pallas_call(functools.partial(forward_kernel, outer, hc, rem), out_sha...  136 us
    pallas_call x1, Pallas kernels, mlp(): pl.pallas_call(functools.partial(mlp_kernel, wide, fc, rem), out_shape=(j...  47.7 us

profile of v1, /device:TPU:11, one launch (start us, length us, event | category | flops | bytes accessed | tf_op | source)
XLA Modules:
  0.0 384.0 jit_solution(17494007197129006832)
XLA Ops:
  0.6 0.0 copy-start
  0.7 0.0 copy-start.7
  0.7 1.4 pad_dynamic-slice_fusion.q_seg
  2.1 0.7 dynamic_slice.27
  2.8 0.7 dynamic_slice.28
  3.6 0.1 fusion.15
  3.7 0.8 dynamic_slice.31
  4.4 0.1 reshape.80
  4.5 0.1 reshape.77
  4.6 0.1 copy.38
  4.7 0.8 fusion.8
  5.5 0.1 copy.41
  5.6 0.9 constant_dynamic-slice_fusion.2
  6.5 0.0 copy-done
  6.6 0.0 copy-done.7
  6.6 0.2 constant_dynamic-slice_fusion.1
  6.8 0.2 copy.47
  7.1 0.0 copy-start.6
  7.1 0.1 copy.50
  7.2 0.2 reshape.79
  7.4 0.1 slice.111
  7.5 0.9 maximum_maximum_fusion.sm
  8.4 0.0 copy-done.6
  8.4 0.1 reshape.73
  8.5 0.1 reshape.74
  8.7 0.1 copy.51
  8.7 0.2 reshape.76
  8.9 0.1 slice.107
  9.0 0.8 maximum_maximum_fusion.1.sa
  9.8 1.1 copy.42.k_seg
  10.9 135.6 %shard_map.271 = (bf16[2,2,272,512]{3,2,1,0:T(8,128)(2,1)}, bf16[8,2,592,512]{3,2,1,0:T(8,128)(2,1)}, bf16[4,1152,1152]{2,1,0:T(8,128)(2,1)}, bf16[1280,1152]{1,...) custom-call(bf16[544,512]{1,0:T(8,128)(2,1)} %bitcast.34, ...), custom_call_target="tpu_custom_call" | custom-call | tf_op jit(solution)/shard_map/pallas_call | solution.py:873
  146.5 47.7 %shard_map.272 = (bf16[8,2,592,512]{3,2,1,0:T(8,128)(2,1)}, bf16[2,544,256]{2,1,0:T(8,128)(2,1)}, f32[256,1152]{1,0:T(8,128)}, f32[16,1152]{1,0:T(8,128)}) custom-call(bf16[256,1152]{1,0:T(8,128)(2,1)} %get-tuple-element.39.low2, bf16[2,2,272,512]{3,2,1,0:T(8,128)(2,1)} %get-tuple-element.40.cot_in, bf16[8,2,592,512]{3,2,1,0:T(8,128)(2,1)} %get-tuple-element.41.gm, ...), custom_call_target="tpu_custom_call" | custom-call | tf_op jit(solution)/shard_map/pallas_call | solution.py:615
  194.2 172.8 %shard_map.273 = (f32[2,592,512]{2,1,0:T(8,128)}, f32[2,304,512]{2,1,0:T(8,128)}, f32[2,544,128]{2,1,0:T(8,128)}, f32[2,272,128]{2,1,0:T(8,128)}, bf16[544,512]{...) custom-call(f32[256,1152]{1,0:T(8,128)} %get-tuple-element.44.grad_r, ...), custom_call_target="tpu_custom_call" | custom-call | tf_op jit(solution)/shard_map/pallas_call | solution.py:1199
  367.0 0.0 copy-start.3
  367.1 0.0 copy-start.2
  367.1 1.3 slice_reduce_fusion.1
  368.3 0.6 reshape_squeeze.10
  369.0 0.6 reshape_squeeze.9
  369.6 1.2 slice_reduce_fusion
  370.9 1.1 fusion.17
  371.9 0.7 reshape_squeeze.11
  372.6 1.7 slice_reduce_fusion.3
  374.3 0.0 copy-done.3
  374.4 0.0 copy-done.2
  374.4 0.1 slice.89
  374.5 0.1 pad_maximum_fusion.2
  374.6 0.5 copy.44
  375.2 0.8 reshape.84
  375.9 0.1 copy.45
  376.0 1.1 reshape.83
  377.1 1.8 fusion.16
  378.9 1.3 pad_maximum_fusion
  380.2 0.0 copy-start.5
  380.2 0.0 copy-start.1
  380.2 1.6 copy.46
  381.7 0.0 copy-start.4
  381.8 0.0 copy-done.5
  381.8 0.8 copy.54
  382.6 0.4 copy-done.4
  383.0 0.8 copy.55
  383.8 0.0 copy-done.1
  (14 shorter events, 0.3 us)
Async XLA Ops:
  0.6 5.9 %copy-start = (bf16[544,544]{1,0:T(8,128)(2,1)S(1)}, bf16[544,544]{1,0:T(8,128)(2,1)}, u32[]{:S(2)}) copy-start(bf16[544,544]{1,0:T(8,128)(2,1)} %param.29) | copy-start | bytes 1775620
  0.7 5.9 %copy-start.7 = (bf16[544,544]{1,0:T(8,128)(2,1)S(1)}, bf16[544,544]{1,0:T(8,128)(2,1)}, u32[]{:S(2)}) copy-start(bf16[544,544]{1,0:T(8,128)(2,1)} %param.27) | copy-start | bytes 1775620
  7.1 1.3 copy-start.6
  367.0 7.3 %copy-start.3 = (f32[2,272,128]{2,1,0:T(8,128)S(1)}, f32[2,272,128]{2,1,0:T(8,128)}, u32[]{:S(2)}) copy-start(f32[2,272,128]{2,1,0:T(8,128)} %get-tuple-element.60) | copy-start | bytes 835588
  367.1 7.3 %copy-start.2 = (f32[2,304,512]{2,1,0:T(8,128)S(1)}, f32[2,304,512]{2,1,0:T(8,128)}, u32[]{:S(2)}) copy-start(f32[2,304,512]{2,1,0:T(8,128)} %get-tuple-element.59) | copy-start | bytes 3735556
  380.2 1.6 copy-start.5
  380.2 3.6 copy-start.1
  381.7 1.3 copy-start.4
